TPU v7x, 256 devices: a whole 4x4x8 slice. The times are simulated.
256 devices in a mesh: seq: 128 (over y_lo, x, z, core), dp: 2 (over y_hi).
Axes of the slice: x: 4, y: 4 (y_hi: 2, y_lo: 2; y = y_hi * 2 + y_lo), z: 8, core: 2. Of those that a mesh axis runs over, the one named last changes fastest.
Arguments:
- inputs: bfloat16 [2, 65536, 512], P('dp', 'seq'), may hold values from -6 to 6
- filter_taps: float32 [6, 2, 512], replicated, may hold values from -3 to 3
- mixing: bfloat16 [6, 512, 512], replicated, may hold values from -0.25 to 0.25
- cotangent: bfloat16 [2, 65536, 512], P('dp', 'seq'), may hold values from -6 to 6
Outputs:
- grad_inputs: float32 [2, 65536, 512], P('dp', 'seq')
- grad_taps: float32 [6, 2, 512], replicated
- grad_mixing: bfloat16 [6, 512, 512], replicated
All inputs are finite; a program needn't handle non-finite values.
Results may differ from a plain program's by a relative error of at most 0.014.
Values may be sent and summed in bfloat16 or wider, within the bound.
A program may use at most 64 MiB of HBM per device.

v0:
```python
import functools, jax, jax.numpy as jnp
from jax import lax
from jax.sharding import PartitionSpec as P
from jax.experimental import pallas as pl
from jax.experimental.pallas import tpu as pltpu
MESH = pl.DeviceIdType.MESH
CHIPS = 64

def coords():
    me = lax.axis_index("seq")
    c = lax.rem(me, 2)
    z = lax.rem(lax.div(me, 2), 8)
    x = lax.rem(lax.div(me, 16), 4)
    w = lax.div(me, 64)
    h = lax.axis_index("dp")
    return h, w, x, z, c

def place(h, w, x, z, c):
    return {"seq": ((w * 4 + x) * 8 + z) * 2 + c, "dp": h}

def on_y(y, x, z, c):
    return place(lax.div(y, 2), lax.rem(y, 2), x, z, c)

def signal(sem, dev):
    pl.semaphore_signal(sem, inc=1, device_id=dev, device_id_type=MESH)

def greet():
    h, w, x, z, c = coords()
    bar = pltpu.get_barrier_semaphore()
    signal(bar, place(h, w, x, z, 1 - c))
    @pl.loop(1, 8)
    def _(k):
        signal(bar, place(h, w, x, lax.rem(z + k, 8), c))
    @pl.loop(1, 4)
    def _(k):
        signal(bar, place(h, w, lax.rem(x + k, 4), z, c))
    y = h * 2 + w
    @pl.loop(1, 4)
    def _(k):
        signal(bar, on_y(lax.rem(y + k, 4), x, z, c))

def meet(plane_sem):
    h, w, x, z, c = coords()
    pl.semaphore_wait(pltpu.get_barrier_semaphore(), 14)
    @pl.loop(1, 4)
    def _(k):
        signal(plane_sem, place(h, w, lax.rem(x + k, 4), z, c))

def enter(plane_sem, all_sem):
    h, w, x, z, c = coords()
    pl.semaphore_wait(plane_sem, 3)
    signal(all_sem, place(h, 1 - w, x, z, c))
    pl.semaphore_wait(all_sem, 1)

def selection(out_of, shape=(256, 256)):
    o = lax.broadcasted_iota(jnp.int32, shape, 0)
    i = lax.broadcasted_iota(jnp.int32, shape, 1)
    return jnp.where(i == out_of(o), 1.0, 0.0).astype(jnp.bfloat16)

def tokens_to_tiles(a_ref, mine, other, c):
    def src(o):
        half, j, cg, n = o // 128, (o // 16) % 8, (o // 4) % 4, o % 4
        return (n * 4 + cg) * 16 + 2 * j + jnp.where(half == 0, c, 1 - c)
    pm = selection(src)
    @pl.loop(0, 8)
    def _(g):
        m = jnp.concatenate([a_ref[pl.ds(pl.multiple_of(n * 128 + g * 16, 16), 16), cg * 128:(cg + 1) * 128] for n in range(4) for cg in range(4)], axis=0)
        t = jnp.dot(pm, m, preferred_element_type=jnp.float32).astype(jnp.bfloat16).reshape(2, 8, 16, 128)
        mine[pl.ds(g * 8, 8), c] = t[0]
        other[pl.ds(g * 8, 8)] = t[1]

def tiles_to_rows(r_ref, put):
    qm = selection(lambda o: ((o // 4) % 16 * 4 + o // 64) * 4 + o % 4)
    @pl.loop(0, 8)
    def _(g):
        m = r_ref[pl.ds(g * 8, 8)].reshape(256, 128)
        t = jnp.dot(qm, m, preferred_element_type=jnp.float32)
        for cg in range(4):
            put(g, cg, t[cg * 64:(cg + 1) * 64])

def rows_to_tiles(g_ref, mine, other, c):
    def src(o):
        half, j, cg, n = o // 128, (o // 16) % 8, (o // 4) % 4, o % 4
        return (cg * 16 + 2 * j + jnp.where(half == 0, c, 1 - c)) * 4 + n
    pm = selection(src)
    @pl.loop(0, 8)
    def _(g):
        m = jnp.concatenate([g_ref[pl.ds(pl.multiple_of(g * 64, 64), 64), cg * 128:(cg + 1) * 128] for cg in range(4)], axis=0)
        t = jnp.dot(pm, m, preferred_element_type=jnp.float32).astype(jnp.bfloat16).reshape(2, 8, 16, 128)
        mine[pl.ds(g * 8, 8), c] = t[0]
        other[pl.ds(g * 8, 8)] = t[1]

def tiles_to_tokens(r_ref, o_ref):
    qm = selection(lambda o: (o % 16 * 4 + (o // 16) % 4) * 4 + o // 64)
    @pl.loop(0, 8)
    def _(g):
        m = r_ref[pl.ds(g * 8, 8)].reshape(256, 128)
        t = jnp.dot(qm, m, preferred_element_type=jnp.float32)
        for n in range(4):
            for cg in range(4):
                o_ref[pl.ds(pl.multiple_of(n * 128 + g * 16, 16), 16), cg * 128:(cg + 1) * 128] = t[(n * 4 + cg) * 16:(n * 4 + cg + 1) * 16]

def pair_copy(other, s_ref, sems, k):
    h, w, x, z, c = coords()
    return pltpu.make_async_remote_copy(other, s_ref.at[:, c], sems.at[0, k], sems.at[1, k], device_id=place(h, w, x, z, 1 - c), device_id_type=MESH)

def spread(s_ref, r_ref, sems, loc, k, begin=1, end=64):
    h, w, x, z, c = coords()
    j = (w * 4 + x) * 8 + z
    if begin == 1:
        pltpu.make_async_copy(s_ref.at[j], r_ref.at[j], loc.at[k]).start()
    @pl.loop(begin, end)
    def _(t):
        b = lax.rem(t, 8)
        a = lax.div(t, 8)
        dz = jnp.where(lax.rem(b, 2) == 1, lax.div(b + 1, 2), 8 - lax.div(b, 2))
        z2 = lax.rem(z + dz, 8)
        x2 = lax.rem(x + lax.rem(a, 4), 4)
        w2 = lax.rem(w + lax.div(a, 4), 2)
        pltpu.make_async_remote_copy(s_ref.at[(w2 * 4 + x2) * 8 + z2], r_ref.at[j], sems.at[0, k], sems.at[1, k], device_id=place(h, w2, x2, z2, c), device_id_type=MESH).start()

def spread_one(s_ref, r_ref, sems, loc, k, core):
    h, w, x, z, c = coords()
    j = (w * 4 + x) * 8 + z
    pltpu.make_async_copy(s_ref.at[j, core], r_ref.at[j, core], loc.at[k]).start()
    @pl.loop(1, 64)
    def _(t):
        b = lax.rem(t, 8)
        a = lax.div(t, 8)
        dz = jnp.where(lax.rem(b, 2) == 1, lax.div(b + 1, 2), 8 - lax.div(b, 2))
        z2 = lax.rem(z + dz, 8)
        x2 = lax.rem(x + lax.rem(a, 4), 4)
        w2 = lax.rem(w + lax.div(a, 4), 2)
        pltpu.make_async_remote_copy(s_ref.at[(w2 * 4 + x2) * 8 + z2, core], r_ref.at[j, core], sems.at[0, k], sems.at[1, k], device_id=place(h, w2, x2, z2, c), device_id_type=MESH).start()

def one_arrived(s_ref, r_ref, sems, loc, k):
    h, w, x, z, c = coords()
    j = (w * 4 + x) * 8 + z
    pltpu.make_async_copy(s_ref.at[j, 0], r_ref.at[j, 0], loc.at[k]).wait()
    some = pl.ds(0, 63)
    pltpu.make_async_copy(s_ref.at[some, 0], r_ref.at[some, 0], sems.at[1, k]).wait()

def one_sent(s_ref, r_ref, sems, k):
    some = pl.ds(0, 63)
    pltpu.make_async_copy(s_ref.at[some, 0], r_ref.at[some, 0], sems.at[0, k]).wait()

def spread_arrived(s_ref, r_ref, sems, loc, k, begin=1, end=64):
    h, w, x, z, c = coords()
    j = (w * 4 + x) * 8 + z
    if begin == 1:
        pltpu.make_async_copy(s_ref.at[j], r_ref.at[j], loc.at[k]).wait()
    some = pl.ds(0, end - begin)
    pltpu.make_async_copy(s_ref.at[some], r_ref.at[some], sems.at[1, k]).wait()

def spread_sent(s_ref, r_ref, sems, k, begin=1, end=64):
    some = pl.ds(0, end - begin)
    pltpu.make_async_copy(s_ref.at[some], r_ref.at[some], sems.at[0, k]).wait()

LEVELS = 6
K0 = 0.7978845608028654
K1C = K0 * 0.044715
PAD = 32
TILE = 128

def forward(l, xf, act, dg, taps_ref, mix_ref):
    d = 1 << l
    for rt in range(512 // TILE):
        r0 = rt * TILE
        for cg in range(4):
            lanes = slice(cg * 128, cg * 128 + 128)
            cur = xf[l, cg, PAD + r0:PAD + r0 + TILE]
            lag = xf[l, cg, PAD + r0 - d:PAD + r0 - d + TILE]
            p = taps_ref[l, 0:1, lanes] * cur + taps_ref[l, 1:2, lanes] * lag
            p2 = p * p
            t = jnp.tanh(p * (K0 + K1C * p2))
            half = 0.5 + 0.5 * t
            act[l, r0:r0 + TILE, lanes] = (p * half).astype(jnp.bfloat16)
            dg[l, cg, r0:r0 + TILE] = half + (half * (1.0 - half) * p) * (2 * K0 + 6 * K1C * p2)
        if l + 1 < LEVELS:
            m = jnp.dot(act[l, r0:r0 + TILE, :], mix_ref[l], preferred_element_type=jnp.float32)
            for cg in range(4):
                nxt = xf[l, cg, PAD + r0:PAD + r0 + TILE] + m[:, cg * 128:cg * 128 + 128]
                xf[l + 1, cg, PAD + r0:PAD + r0 + TILE] = nxt.astype(jnp.bfloat16).astype(jnp.float32)

def backward(l, xf, dg, g, gb, lag, taps_ref, mix_ref, gtaps):
    d = 1 << l
    sums = [[jnp.zeros((8, 128), jnp.float32) for _ in range(2)] for _ in range(4)]
    for rt in reversed(range(512 // TILE)):
        r0 = rt * TILE
        ga = lax.dot_general(gb[r0:r0 + TILE, :], mix_ref[l], (((1,), (1,)), ((), ())), preferred_element_type=jnp.float32)
        for cg in range(4):
            lanes = slice(cg * 128, cg * 128 + 128)
            gp = ga[:, lanes] * dg[l, cg, r0:r0 + TILE]
            cur = xf[l, cg, PAD + r0:PAD + r0 + TILE]
            old = xf[l, cg, PAD + r0 - d:PAD + r0 - d + TILE]
            sums[cg][0] += jnp.sum((gp * cur).reshape(TILE // 8, 8, 128), axis=0)
            sums[cg][1] += jnp.sum((gp * old).reshape(TILE // 8, 8, 128), axis=0)
            lag[cg, r0:r0 + TILE] = (taps_ref[l, 1:2, lanes] * gp).astype(jnp.bfloat16).astype(jnp.float32)
            new = g[cg, r0:r0 + TILE] + taps_ref[l, 0:1, lanes] * gp + lag[cg, r0 + d:r0 + d + TILE]
            g[cg, r0:r0 + TILE] = new
            gb[r0:r0 + TILE, lanes] = new.astype(jnp.bfloat16)
    for cg in range(4):
        for k in range(2):
            gtaps[2 * l + k:2 * l + k + 1, cg * 128:cg * 128 + 128] = jnp.sum(sums[cg][k], axis=0, keepdims=True)

def mix_grad(l, act, gb):
    return lax.dot_general(act[l], gb[...], (((0,), (0,)), ((), ())), preferred_element_type=jnp.float32)


VM = pl.BlockSpec(memory_space=pltpu.VMEM)

class Reduction:
    def __init__(self, gm, final, out, c0, hh, r1, qq, r2, e8, r3, f8, ss, rs, ls):
        self.__dict__.update(gm=gm, final=final, out=out, ls=ls, c0=c0, hh=hh, r1=r1, qq=qq, r2=r2, e8=e8, r3=r3, f8=f8, ss=ss, rs=rs)
        self.h, self.w, self.x, self.z, self.c = h, w, x, z, c = coords()
        self.y = h * 2 + w
        others = lambda i, n: [lax.rem(i + k, n) for k in sorted(range(1, n), key=lambda k: -min(k, n - k))]
        self.on_axis = {1: [(j, place(h, w, j, z, c)) for j in others(x, 4)], 0: [(j, on_y(j, x, z, c)) for j in others(self.y, 4)]}
        self.on_z = [(j, place(h, w, x, j, c)) for j in others(z, 8)]

    def first(self, l):
        return self.x if l % 2 else self.y

    def second(self, l):
        return self.y if l % 2 else self.x

    def copy(self, src, dst, l, stage, dev):
        return pltpu.make_async_remote_copy(src, dst, self.ss.at[l, stage], self.rs.at[l, stage], device_id=dev, device_id_type=MESH)

    def other_core(self):
        return place(self.h, self.w, self.x, self.z, 1 - self.c)

    def rows(self, l):
        r256 = self.c * 256
        r64 = r256 + self.first(l) * 64
        return pl.multiple_of(r256, 256), pl.multiple_of(r64, 64), pl.multiple_of(r64 + self.second(l) * 16, 16)

    def took(self, ref, l, stage):
        pltpu.make_async_copy(ref, ref, self.rs.at[l, stage]).wait()

    def gave(self, ref, l, stage):
        pltpu.make_async_copy(ref, ref, self.ss.at[l, stage]).wait()

    def halve(self, l):
        far = pl.multiple_of((1 - self.c) * 256, 256)
        self.copy(self.gm.at[l, pl.ds(far, 256)], self.c0.at[l], l, 0, self.other_core()).start()

    def quarter(self, l):
        self.took(self.c0.at[l], l, 0)
        near = self.rows(l)[0]
        self.hh[l] = (self.gm[l, pl.ds(near, 256)].astype(jnp.float32) + self.c0[l].astype(jnp.float32)).astype(jnp.bfloat16)
        i = self.first(l)
        for j, dev in self.on_axis[l % 2]:
            self.copy(self.hh.at[l, pl.ds(pl.multiple_of(j * 64, 64), 64)], self.r1.at[l, i], l, 1, dev).start()

    def sixteenth(self, l):
        self.took(self.r1.at[l, pl.ds(0, 3)], l, 1)
        i = self.first(l)
        s = self.hh[l, pl.ds(pl.multiple_of(i * 64, 64), 64)].astype(jnp.float32)
        for k in range(1, 4):
            s += self.r1[l, lax.rem(i + k, 4)].astype(jnp.float32)
        self.qq[l] = s.astype(jnp.bfloat16)
        i2 = self.second(l)
        for j, dev in self.on_axis[1 - l % 2]:
            self.copy(self.qq.at[l, pl.ds(pl.multiple_of(j * 16, 16), 16)], self.r2.at[l, i2], l, 2, dev).start()

    def tile(self, p):
        z = self.z
        for l in (2 * p, 2 * p + 1):
            self.took(self.r2.at[l, pl.ds(0, 3)], l, 2)
            i2 = self.second(l)
            s = self.qq[l, pl.ds(pl.multiple_of(i2 * 16, 16), 16)].astype(jnp.float32)
            for k in range(1, 4):
                s += self.r2[l, lax.rem(i2 + k, 4)].astype(jnp.float32)
            for cg in range(4):
                self.e8[p, l % 2 * 4 + cg] = s[:, cg * 128:cg * 128 + 128].astype(jnp.bfloat16)
        for j, dev in self.on_z:
            self.copy(self.e8.at[p, j], self.r3.at[p, z], 2 * p, 3, dev).start()

    def untile(self, p):
        z = self.z
        self.took(self.r3.at[p, pl.ds(0, 7)], 2 * p, 3)
        s = self.e8[p, z].astype(jnp.float32)
        for k in range(1, 8):
            s += self.r3[p, lax.rem(z + k, 8)].astype(jnp.float32)
        self.f8[p, z] = s.astype(jnp.bfloat16)
        for j, dev in self.on_z:
            self.copy(self.f8.at[p, z], self.f8.at[p, z], 2 * p, 4, dev).start()

    def unsixteenth(self, p):
        self.took(self.f8.at[p, pl.ds(0, 7)], 2 * p, 4)
        for l in (2 * p, 2 * p + 1):
            r16 = self.rows(l)[2]
            for cg in range(4):
                self.out[l, pl.ds(r16, 16), cg * 128:cg * 128 + 128] = self.f8[p, l % 2 * 4 + cg]
            mine = self.out.at[l, pl.ds(r16, 16)]
            for j, dev in self.on_axis[1 - l % 2]:
                self.copy(mine, mine, l, 5, dev).start()

    def unquarter(self, p):
        for l in (2 * p, 2 * p + 1):
            self.took(self.out.at[l, pl.ds(0, 48)], l, 5)
            mine = self.out.at[l, pl.ds(self.rows(l)[1], 64)]
            for j, dev in self.on_axis[l % 2]:
                self.copy(mine, mine, l, 6, dev).start()

    def unhalve(self, p):
        for l in (2 * p, 2 * p + 1):
            self.took(self.out.at[l, pl.ds(0, 192)], l, 6)
            mine = self.out.at[l, pl.ds(self.rows(l)[0], 256)]
            there = self.final.at[l, pl.ds(self.rows(l)[0], 256)]
            self.copy(mine, there, l, 7, self.other_core()).start()
            pltpu.make_async_copy(mine, there, self.ls.at[l]).start()

    def settle(self, p):
        for l in (2 * p, 2 * p + 1):
            self.gave(self.c0.at[l], l, 0)
            self.gave(self.r1.at[l, pl.ds(0, 3)], l, 1)
            self.gave(self.r2.at[l, pl.ds(0, 3)], l, 2)
            self.gave(self.out.at[l, pl.ds(0, 48)], l, 5)
            self.gave(self.out.at[l, pl.ds(0, 192)], l, 6)
        self.gave(self.r3.at[p, pl.ds(0, 7)], 2 * p, 3)
        self.gave(self.f8.at[p, pl.ds(0, 7)], 2 * p, 4)

    def finish(self, p):
        for l in (2 * p, 2 * p + 1):
            half = self.final.at[l, pl.ds(0, 256)]
            pltpu.make_async_copy(half, half, self.ls.at[l]).wait()
            self.gave(self.out.at[l, pl.ds(0, 256)], l, 7)
            self.took(half, l, 7)

class TapSums:
    def __init__(self, bufs, ss, rs):
        self.pair, self.quarters, *self.slots, self.done = bufs
        self.ss, self.rs = ss, rs
        self.h, self.w, self.x, self.z, self.c = coords()
        self.y = self.h * 2 + self.w

    def others(self, stage):
        h, w, x, z, c = self.h, self.w, self.x, self.z, self.c
        if stage == 0:
            return [(1 - c, place(h, w, x, z, 1 - c))]
        if stage in (1, 4):
            return [(j, place(h, w, j, z, c)) for j in (lax.rem(x + k, 4) for k in range(1, 4))]
        if stage == 2:
            return [(j, on_y(j, x, z, c)) for j in (lax.rem(self.y + k, 4) for k in range(1, 4))]
        return [(j, place(h, w, x, j, c)) for j in (lax.rem(z + k, 8) for k in range(1, 8))]

    def buf(self, stage):
        return (self.pair, *self.slots, self.done)[stage]

    def push(self, stage, i, src):
        for j, dev in self.others(stage):
            pltpu.make_async_remote_copy(src(j), self.buf(stage).at[i], self.ss.at[stage], self.rs.at[stage], device_id=dev, device_id_type=MESH).start()

    def send(self, stage, value):
        i = (self.c, self.x, self.y, self.z, self.x)[stage]
        buf = self.buf(stage)
        if stage == 1:
            for q in range(4):
                self.quarters[q] = value[:, q * 128:q * 128 + 128]
            buf[i] = self.quarters[i]
            self.push(1, i, lambda j: self.quarters.at[j])
        else:
            buf[i] = value
            self.push(stage, i, lambda j: buf.at[i])

    def came(self, stage):
        buf = self.buf(stage)
        part = buf.at[pl.ds(0, buf.shape[0] - 1)]
        pltpu.make_async_copy(part, part, self.rs.at[stage]).wait()

    def total(self, stage):
        self.came(stage)
        buf = self.buf(stage)
        s = buf[0]
        for k in range(1, buf.shape[0]):
            s += buf[k]
        return s

    def result(self, out):
        self.came(4)
        for q in range(4):
            out[:, q * 128:q * 128 + 128] = self.done[q]

    def finish(self):
        for stage in range(5):
            buf = self.buf(stage)
            part = buf.at[pl.ds(0, buf.shape[0] - 1)]
            pltpu.make_async_copy(part, part, self.ss.at[stage]).wait()

def reduction_scratch():
    b = lambda *s: pltpu.VMEM(s, jnp.bfloat16)
    D = pltpu.SemaphoreType.DMA
    return [b(6, 512, 512), b(6, 512, 512), b(6, 256, 512), b(6, 256, 512), b(6, 4, 64, 512), b(6, 64, 512), b(6, 4, 16, 512), b(3, 8, 16, 128), b(3, 8, 16, 128), b(3, 8, 16, 128), D((6, 8)), D((6, 8)), D((6,))]

def tap_scratch():
    D = pltpu.SemaphoreType.DMA
    return [pltpu.VMEM((2, 16, 512), jnp.float32)] + [pltpu.VMEM((n, 16, 128), jnp.float32) for n in (4, 4, 4, 8, 4)] + [D((5,)), D((5,))]

def entry_scratch():
    return [pltpu.SemaphoreType.REGULAR] * 2


def kernel(x_hbm, c_hbm, taps_ref, mix_hbm, o_hbm, gt_out, gm_out, *scratch):
    scratch = list(scratch)
    def take(n):
        got = scratch[:n]
        del scratch[:n]
        return got
    x_ref, c_ref, mix_ref, in_sems = take(4)
    ox, sx, rx, oc, sc, rc, og, sg, rg, tok = take(10)
    pair_sems, sems, loc = take(3)
    xf, act, dg, g, gb, lag, gt = take(7)
    gm, *rest = take(13)
    red = Reduction(gm, gm_out, *rest)
    *bufs, tss, trs = take(8)
    taps = TapSums(bufs, tss, trs)
    plane_sem, all_sem = take(2)
    h, w, x, z, c = coords()

    greet()
    loads = [pltpu.make_async_copy(s, d, in_sems.at[i]) for i, (s, d) in enumerate(((x_hbm, x_ref), (c_hbm, c_ref), (mix_hbm, mix_ref)))]
    for load in loads:
        load.start()
    xf[:, :, 0:PAD] = jnp.zeros((LEVELS, 4, PAD, 128), jnp.float32)
    lag[:, 512:512 + PAD] = jnp.zeros((4, PAD, 128), jnp.float32)
    gt[...] = jnp.zeros((16, 512), jnp.float32)
    meet(plane_sem)
    loads[0].wait()
    tokens_to_tiles(x_ref, sx, ox, c)
    enter(plane_sem, all_sem)
    px = pair_copy(ox, sx, pair_sems, 0)
    px.start()
    spread_one(sx, rx, sems, loc, 0, c)
    loads[1].wait()
    tokens_to_tiles(c_ref, sc, oc, c)
    pc = pair_copy(oc, sc, pair_sems, 1)
    pc.start()
    px.wait_recv()
    spread_one(sx, rx, sems, loc, 3, 1 - c)
    one_arrived(sx, rx, sems, loc, 0)
    pc.wait_recv()
    spread(sc, rc, sems, loc, 1)
    loads[2].wait()
    one_arrived(sx, rx, sems, loc, 3)
    def put_x(i, cg, t):
        xf[0, cg, pl.ds(pl.multiple_of(PAD + i * 64, 32), 64)] = t
    tiles_to_rows(rx, put_x)
    for l in range(LEVELS):
        forward(l, xf, act, dg, taps_ref, mix_ref)

    spread_arrived(sc, rc, sems, loc, 1)
    def put_c(i, cg, t):
        rows = pl.ds(pl.multiple_of(i * 64, 64), 64)
        g[cg, rows] = t
        gb[rows, cg * 128:cg * 128 + 128] = t.astype(jnp.bfloat16)
    tiles_to_rows(rc, put_c)

    for l in reversed(range(LEVELS)):
        gm[l] = mix_grad(l, act, gb).astype(jnp.bfloat16)
        red.halve(l)
        backward(l, xf, dg, g, gb, lag, taps_ref, mix_ref, gt)
        if l == 3:
            red.quarter(5)
            red.quarter(4)
        if l == 2:
            red.quarter(3)
        if l == 1:
            red.quarter(2)

    rows_to_tiles(gb, sg, og, c)
    pg = pair_copy(og, sg, pair_sems, 2)
    pg.start()
    red.sixteenth(5)
    red.sixteenth(4)
    red.sixteenth(3)
    red.quarter(0)
    red.sixteenth(2)
    red.quarter(1)
    taps.send(0, gt[...])
    red.tile(2)
    pg.wait_recv()
    spread(sg, rg, sems, loc, 2, 1, 8)
    red.tile(1)
    spread(sg, rg, sems, loc, 2, 8, 16)
    red.sixteenth(0)
    taps.send(1, taps.total(0))
    red.sixteenth(1)
    red.untile(2)
    spread(sg, rg, sems, loc, 2, 16, 24)
    red.untile(1)
    red.tile(0)
    spread(sg, rg, sems, loc, 2, 24, 32)
    red.unsixteenth(2)
    spread(sg, rg, sems, loc, 2, 32, 40)
    spread(sg, rg, sems, loc, 2, 40, 48)
    red.unsixteenth(1)
    red.unquarter(2)
    red.untile(0)
    spread(sg, rg, sems, loc, 2, 48, 56)
    taps.send(2, taps.total(1))
    spread(sg, rg, sems, loc, 2, 56, 64)
    red.unsixteenth(0)
    red.unquarter(1)
    taps.send(3, taps.total(2))
    red.unhalve(2)
    red.unquarter(0)
    red.unhalve(1)
    spread_arrived(sg, rg, sems, loc, 2)
    tiles_to_tokens(rg, tok)
    tokens = pltpu.make_async_copy(tok, o_hbm, in_sems.at[0])
    tokens.start()
    taps.send(4, taps.total(3))
    red.unhalve(0)
    taps.result(gt_out)
    taps.finish()
    px.wait_send()
    pc.wait_send()
    pg.wait_send()
    one_sent(sx, rx, sems, 0)
    one_sent(sx, rx, sems, 3)
    spread_sent(sc, rc, sems, 1)
    spread_sent(sg, rg, sems, 2)
    for p in (2, 1, 0):
        red.settle(p)
    tokens.wait()
    for p in (2, 1, 0):
        red.finish(p)

def finish(o, gt, gm, o_out, gt_out, gm_out, held_o, held, sems, o_sems):
    ins = [pltpu.make_async_copy(gm.at[l], held.at[l], sems.at[0, l]) for l in range(LEVELS)]
    outs = [pltpu.make_async_copy(held.at[l], gm_out.at[l], sems.at[1, l]) for l in range(LEVELS)]
    for i in range(2):
        rows = pl.ds(i * 256, 256)
        ins.append(pltpu.make_async_copy(o.at[rows], held_o.at[rows], o_sems.at[0, i]))
        outs.append(pltpu.make_async_copy(held_o.at[rows], o_out.at[rows], o_sems.at[1, i]))
    for move in ins:
        move.start()
    for l in range(LEVELS):
        gt_out[l] = gt[2 * l:2 * l + 2]
    for i, move in enumerate(ins):
        move.wait()
        outs[i].start()
    for move in outs:
        move.wait()

def local(inputs, filter_taps, mixing, cotangent):
    f, b = jnp.float32, jnp.bfloat16
    V, S, D = pltpu.VMEM, jax.ShapeDtypeStruct, pltpu.SemaphoreType.DMA
    ANY = pl.BlockSpec(memory_space=pl.ANY)
    loaded = [V((512, 512), b), V((512, 512), b), V((LEVELS, 512, 512), b), D((3,))]
    exchange = ([V((64, 16, 128), b), V((64, 2, 16, 128), b), V((64, 2, 16, 128), b)] * 3) + [V((512, 512), f), D((2, 3)), D((2, 4)), D((4,))]
    levels = [V((LEVELS, 4, PAD + 512, 128), f), V((LEVELS, 512, 512), b), V((LEVELS, 4, 512, 128), f), V((4, 512, 128), f), V((512, 512), b), V((4, 512 + PAD, 128), f), V((16, 512), f)]
    o, gt, gm = pl.pallas_call(
        kernel,
        out_shape=[S((512, 512), f), S((16, 512), f), S((LEVELS, 512, 512), b)],
        in_specs=[ANY, ANY, VM, ANY],
        out_specs=[ANY, VM, ANY],
        scratch_shapes=loaded + exchange + levels + reduction_scratch() + tap_scratch() + entry_scratch(),
        compiler_params=pltpu.CompilerParams(collective_id=1, has_side_effects=True, vmem_limit_bytes=60 << 20),
        cost_estimate=pl.CostEstimate(flops=4831838208, bytes_accessed=10 << 20, transcendentals=1572864),
    )(inputs[0], cotangent[0], filter_taps, mixing)
    o, gt, gm = pl.pallas_call(
        finish,
        out_shape=[S((512, 512), f), S((LEVELS, 2, 512), f), S((LEVELS, 512, 512), b)],
        in_specs=[ANY, VM, ANY],
        out_specs=[ANY, VM, ANY],
        scratch_shapes=[V((512, 512), f), V((LEVELS, 512, 512), b), D((2, LEVELS)), D((2, 2))],
        compiler_params=pltpu.CompilerParams(vmem_limit_bytes=60 << 20),
    )(o, gt, gm)
    return o[None], gt, gm

def solution(mesh):
    halves = P("dp", "seq", None)
    return jax.shard_map(local, mesh=mesh, in_specs=(halves, P(), P(), halves), out_specs=(halves, P(), P()), check_vma=False)
```

profile of v0, /device:TPU:1, one launch (start us, length us, event | category | flops | bytes accessed | tf_op | source)
XLA Modules:
  0.0 93.2 jit_solution(16859593873987323482)
XLA Ops:
  0.6 87.5 %shard_map.67 = (f32[512,512]{1,0:T(8,128)}, f32[16,512]{1,0:T(8,128)}, bf16[6,512,512]{2,1,0:T(8,128)(2,1)}) custom-call(bf16[512,512]{1,0:T(8,128)(2,1)} %bitcast.4, bf16[512,512]{1,0:T(8,128)(2,1)} %bitcast.5, f32[6,2,512]{2,1,0:T(2,128)} %taps_ref.1, bf16[6,512,512]{2,1,0:T(8,128)(2,1)} %mix_hbm.1), custom_call_target="tpu_custom_call" | custom-call | flops 4831838208 | bytes 10485760 | tf_op jit(solution)/shard_map/pallas_call | solution.py:555
  88.1 4.9 %shard_map.68 = (f32[512,512]{1,0:T(8,128)}, f32[6,2,512]{2,1,0:T(2,128)}, bf16[6,512,512]{2,1,0:T(8,128)(2,1)}) custom-call(f32[512,512]{1,0:T(8,128)} %get-tuple-element.9.o, f32[16,512]{1,0:T(8,128)} %get-tuple-element.10.gt, bf16[6,512,512]{2,1,0:T(8,128)(2,1)} %get-tuple-element.11.gm), custom_call_target="tpu_custom_call" | custom-call | tf_op jit(solution)/shard_map/pallas_call | solution.py:564
where the time goes:
time: 93.4 us; the launch traced here: 93.2 us
  Pallas kernels  92.4 us (99%)
    pallas_call x1, Pallas kernels, local(): pl.pallas_call(kernel, out_shape=[S((512, 512), f), S((16, 512), f), S((L...  87.5 us
    pallas_call x1, Pallas kernels, local(): pl.pallas_call(finish, out_shape=[S((512, 512), f), S((LEVELS, 2, 512), f...  4.94 us

commit v1 on v0

--- a/solution.py
+++ b/solution.py
@@ -469,20 +469,20 @@
         if l == 1:
             red.quarter(2)
 
+    red.sixteenth(5)
+    red.sixteenth(4)
+    red.sixteenth(3)
+    red.quarter(1)
+    red.quarter(0)
+    red.sixteenth(2)
     rows_to_tiles(gb, sg, og, c)
     pg = pair_copy(og, sg, pair_sems, 2)
     pg.start()
-    red.sixteenth(5)
-    red.sixteenth(4)
-    red.sixteenth(3)
-    red.quarter(0)
-    red.sixteenth(2)
-    red.quarter(1)
     taps.send(0, gt[...])
     red.tile(2)
+    red.tile(1)
     pg.wait_recv()
     spread(sg, rg, sems, loc, 2, 1, 8)
-    red.tile(1)
     spread(sg, rg, sems, loc, 2, 8, 16)
     red.sixteenth(0)
     taps.send(1, taps.total(0))

time: 93.4 us -> 94.4 us (1.011)
  Pallas kernels: 92.4 us -> 93.4 us
    pallas_call x1, Pallas kernels: 87.5 us -> 88.5 us  [local(): pl.pallas_call(kernel, out_shape=[S((512, 512), f), S((16, 512), f), S((L...]
where the time goes in v1:
time: 94.4 us; the launch traced here: 94.2 us
  Pallas kernels  93.4 us (99%)
    pallas_call x1, Pallas kernels, local(): pl.pallas_call(kernel, out_shape=[S((512, 512), f), S((16, 512), f), S((L...  88.5 us
    pallas_call x1, Pallas kernels, local(): pl.pallas_call(finish, out_shape=[S((512, 512), f), S((LEVELS, 2, 512), f...  4.94 us

profile of v1, /device:TPU:1, one launch (start us, length us, event | category | flops | bytes accessed | tf_op | source)
XLA Modules:
  0.0 94.2 jit_solution(17145944494751138537)
XLA Ops:
  0.6 88.5 %shard_map.67 = (f32[512,512]{1,0:T(8,128)}, f32[16,512]{1,0:T(8,128)}, bf16[6,512,512]{2,1,0:T(8,128)(2,1)}) custom-call(bf16[512,512]{1,0:T(8,128)(2,1)} %bitcast.4, bf16[512,512]{1,0:T(8,128)(2,1)} %bitcast.5, f32[6,2,512]{2,1,0:T(2,128)} %taps_ref.1, bf16[6,512,512]{2,1,0:T(8,128)(2,1)} %mix_hbm.1), custom_call_target="tpu_custom_call" | custom-call | flops 4831838208 | bytes 10485760 | tf_op jit(solution)/shard_map/pallas_call | solution.py:555
  89.1 4.9 %shard_map.68 = (f32[512,512]{1,0:T(8,128)}, f32[6,2,512]{2,1,0:T(2,128)}, bf16[6,512,512]{2,1,0:T(8,128)(2,1)}) custom-call(f32[512,512]{1,0:T(8,128)} %get-tuple-element.9.o, f32[16,512]{1,0:T(8,128)} %get-tuple-element.10.gt, bf16[6,512,512]{2,1,0:T(8,128)(2,1)} %get-tuple-element.11.gm), custom_call_target="tpu_custom_call" | custom-call | tf_op jit(solution)/shard_map/pallas_call | solution.py:564
